TPU v7x, 32 devices: a whole 2x2x4 slice. The times are simulated.
32 devices in a mesh: design: 2 (over y), cluster: 4 (over z), blk: 2 (over x), sub: 2 (over core).
Axes of the slice: x: 2, y: 2, z: 4, core: 2. Of those that a mesh axis runs over, the one named last changes fastest.
Arguments:
- density: bfloat16 [16, 256, 256], P(('design', 'cluster')), parts along dimension 0, may hold values from -6 to 6
- far_cols: int32 [256], P(('design', 'cluster', 'blk', 'sub')), parts along dimension 0, may hold values from 0 to 1
- far_bucket: int32 [256], P(('design', 'cluster', 'blk', 'sub')), parts along dimension 0, may hold values from 0 to 4
- far_v: bfloat16 [256, 64, 256], P(('design', 'cluster', 'blk', 'sub')), parts along dimension 0, may hold values from -0.375 to 0.375
- far_u: bfloat16 [256, 64, 256], P(('design', 'cluster', 'blk', 'sub')), parts along dimension 0, may hold values from -0.1875 to 0.1875
- near_rows: int32 [64], P(('design', 'cluster', 'blk', 'sub')), parts along dimension 0, may hold values from 0 to 1
- near_cols: int32 [64], P(('design', 'cluster', 'blk', 'sub')), parts along dimension 0, may hold values from 0 to 5
- near_tiles: bfloat16 [64, 256, 256], P(('design', 'cluster', 'blk', 'sub')), parts along dimension 0, may hold values from -0.125 to 0.125
- ag_leaf: int32 [8192], P(('design', 'cluster', 'blk', 'sub')), parts along dimension 0, may hold values from 0 to 1
- ag_grad: bfloat16 [8192, 3, 256], P(('design', 'cluster', 'blk', 'sub')), parts along dimension 0, may hold values from -0.375 to 0.375
- ag_normal: float32 [6, 4096], P('design', ('cluster', 'blk', 'sub')), parts along dimension 0, may hold values from -5 to 5
- ag_arm: float32 [6, 4096], P('design', ('cluster', 'blk', 'sub')), parts along dimension 0, may hold values from -5 to 5
- ag_area: float32 [8192], P(('design', 'cluster', 'blk', 'sub')), parts along dimension 0, may hold values from 0.002 to 0.02
Outputs:
- potential: bfloat16 [16, 256, 256], P(('design', 'cluster')), parts along dimension 0
- sector_force: float32 [16, 3, 256], P(('design', 'cluster')), parts along dimension 0
- torque: float32 [6, 256], P('design'), parts along dimension 0
There are 2 independent parts, one for each index of `design`. A program takes and returns all parts, laid end to end along the dimension named above; each array names one. Nothing has to cross between parts.
All inputs are finite; a program needn't handle non-finite values.
Results may differ from a plain program's by a relative error of at most 0.0066.
Values may be sent and summed in bfloat16 or wider, within the bound.
A program may use at most 64 MiB of HBM per device.

v0:
```python
import math
import jax
import jax.numpy as jnp
from jax import lax
from jax.sharding import PartitionSpec as P


def padded(block, sides, width):
    for axis, dim in sides:
        count = lax.axis_size(axis)
        forward = [(i, i + 1) for i in range(count - 1)]
        forward.append((count - 1, 0))
        backward = [(target, source) for source, target in forward]
        low = lax.ppermute(
            lax.slice_in_dim(block, block.shape[dim] - width, None, axis=dim), axis, forward
        )
        high = lax.ppermute(lax.slice_in_dim(block, 0, width, axis=dim), axis, backward)
        block = jnp.concatenate([low, block, high], axis=dim)
    return block


def rank_table(bucket, rank_dim):
    widths = rank_dim // jnp.left_shift(jnp.int32(1), 4 - bucket) * (bucket > 0).astype(jnp.int32)
    return jnp.arange(rank_dim, dtype=jnp.int32)[None, :] < widths[:, None]


def surface_stress(phi_local, leaf_ids, grad_rows, normals, arms, areas):
    groups, panels, loads = phi_local.shape
    count = leaf_ids.shape[0]
    field_h = jnp.zeros((count, 3, loads), jnp.float32)
    for leaf_idx in range(groups):
        values = jnp.dot(
            grad_rows.reshape(count * 3, panels),
            phi_local[leaf_idx],
            preferred_element_type=jnp.float32,
        )
        field_h = field_h + jnp.where(
            (leaf_ids == leaf_idx)[:, None, None], values.reshape(count, 3, loads), 0.0
        )
    normal_t = jnp.transpose(normals)[:, :, None]
    along = jnp.sum(field_h * normal_t, axis=1)
    squared = jnp.sum(field_h * field_h, axis=1)
    traction = along[:, None, :] * field_h - 0.5 * squared[:, None, :] * normal_t
    weighted = traction * areas[:, None, None]
    sectors = jnp.stack(
        [
            jnp.sum(jnp.where((leaf_ids == leaf_idx)[:, None, None], weighted, 0.0), axis=0)
            for leaf_idx in range(groups)
        ]
    )
    arm_t = jnp.transpose(arms)[:, :, None]
    moment_x = jnp.sum(arm_t[:, 1] * weighted[:, 2] - arm_t[:, 2] * weighted[:, 1], axis=0)
    moment_y = jnp.sum(arm_t[:, 2] * weighted[:, 0] - arm_t[:, 0] * weighted[:, 2], axis=0)
    moment_z = jnp.sum(arm_t[:, 0] * weighted[:, 1] - arm_t[:, 1] * weighted[:, 0], axis=0)
    return (sectors, jnp.stack([moment_x, moment_y, moment_z]))


def far_field(field, far_cols, far_bucket, far_v, far_u):
    owners = lax.axis_size("cluster")
    groups, panels, loads = field.shape
    rank_dim = far_v.shape[1]
    picked = jnp.take(field, far_cols, axis=0)
    coeffs = jnp.einsum("srl,sln->srn", far_v, picked, preferred_element_type=jnp.float32)
    coeffs = jnp.where(rank_table(far_bucket, rank_dim)[:, :, None], coeffs, 0.0).astype(
        jnp.bfloat16
    )
    coeffs = coeffs.reshape(owners, groups, rank_dim, loads)
    basis = far_u.reshape(owners, groups, rank_dim, panels)
    arrived = lax.all_to_all(coeffs, "cluster", split_axis=0, concat_axis=0, tiled=True)
    return jnp.einsum("bqrl,bqrn->qln", basis, arrived, preferred_element_type=jnp.float32)


def near_field(field, near_rows, near_cols, near_tiles):
    groups = field.shape[0]
    extended = padded(field, (("cluster", 0),), groups)
    picked = jnp.take(extended, near_cols, axis=0)
    values = jnp.einsum("kij,kjn->kin", near_tiles, picked, preferred_element_type=jnp.float32)
    onehot = near_rows[:, None] == jnp.arange(groups, dtype=jnp.int32)[None, :]
    return jnp.sum(jnp.where(onehot[:, :, None, None], values[:, None], 0.0), axis=0)


def apply_operator(field, far_cols, far_bucket, far_v, far_u, near_rows, near_cols, near_tiles):
    partial_sum = far_field(field, far_cols, far_bucket, far_v, far_u) + near_field(
        field, near_rows, near_cols, near_tiles
    )
    summed = lax.psum(partial_sum, ("blk", "sub"))
    return (0.5 * field.astype(jnp.float32) + summed).astype(jnp.bfloat16)


def per_device(
    density,
    far_cols,
    far_bucket,
    far_v,
    far_u,
    near_rows,
    near_cols,
    near_tiles,
    ag_leaf,
    ag_grad,
    ag_normal,
    ag_arm,
    ag_area,
):
    first = apply_operator(
        density, far_cols, far_bucket, far_v, far_u, near_rows, near_cols, near_tiles
    )
    potential = apply_operator(
        first, far_cols, far_bucket, far_v, far_u, near_rows, near_cols, near_tiles
    )
    sector_part, torque_part = surface_stress(
        potential, ag_leaf, ag_grad, ag_normal, ag_arm, ag_area
    )
    scale = 1.0 / math.sqrt(lax.axis_size("cluster") * lax.axis_size("blk") * lax.axis_size("sub"))
    sector_force = lax.psum(sector_part, ("blk", "sub"))
    torque = lax.psum(torque_part, ("cluster", "blk", "sub"))
    return (potential, sector_force, torque * scale)


def solution(mesh):
    placed = (
        P(("design", "cluster"), None, None),
        P(("design", "cluster", "blk", "sub")),
        P(("design", "cluster", "blk", "sub")),
        P(("design", "cluster", "blk", "sub"), None, None),
        P(("design", "cluster", "blk", "sub"), None, None),
        P(("design", "cluster", "blk", "sub")),
        P(("design", "cluster", "blk", "sub")),
        P(("design", "cluster", "blk", "sub"), None, None),
        P(("design", "cluster", "blk", "sub")),
        P(("design", "cluster", "blk", "sub"), None, None),
        P("design", ("cluster", "blk", "sub")),
        P("design", ("cluster", "blk", "sub")),
        P(("design", "cluster", "blk", "sub")),
    )
    return jax.shard_map(
        per_device,
        mesh=mesh,
        in_specs=placed,
        out_specs=(
            P(("design", "cluster"), None, None),
            P(("design", "cluster"), None, None),
            P("design", None),
        ),
        check_vma=False,
    )
```

profile of v0, /device:TPU:0, one launch (start us, length us, event | category | flops | bytes accessed | tf_op | source)
XLA Modules:
  0.0 175.1 jit_solution(4676703497687636807)
XLA Ops:
  7.2 3.1 %collective-permute-start = (bf16[2,256,256]{2,1,0:T(8,128)(2,1)}, bf16[2,256,256]{2,1,0:T(8,128)(2,1)S(1)}, u32[]{:S(2)}, u32[]{:S(2)}) collective-permute-start(bf16[2,256,256]{2,1,0:T(8,128)(2,1)} %param.17), channel_id=1, source_target_pairs={{0,4},{4,8},{8,12},{12,0},{1,5},{5,9},{9,13},{13,1},{2,6},{6,10},{... | collective-permute-start | bytes 786440 | tf_op jit(solution)/shard_map/ppermute | solution.py:14
  10.3 2.1 %collective-permute-start.1 = (bf16[2,256,256]{2,1,0:T(8,128)(2,1)}, bf16[2,256,256]{2,1,0:T(8,128)(2,1)S(1)}, u32[]{:S(2)}, u32[]{:S(2)}) collective-permute-start(bf16[2,256,256]{2,1,0:T(8,128)(2,1)} %param.17), channel_id=1, source_target_pairs={{4,0},{8,4},{12,8},{0,12},{5,1},{9,5},{13,9},{1,13},{6,2},{10,6},{... | collective-permute-start | bytes 786440 | tf_op jit(solution)/shard_map/ppermute | solution.py:17
  12.4 0.7 compare_select_fusion.1
  13.1 1.6 gather_fusion
  14.7 0.1 compare_select_fusion.2
  14.8 0.1 iota_compare_fusion
  14.9 1.1 fusion.12
  16.0 3.5 %all-to-all-start = ((bf16[4,2,64,256]{3,2,1,0:T(8,128)(2,1)}), bf16[4,2,64,256]{3,2,1,0:T(8,128)(2,1)S(1)}, u32[]{:S(2)}, u32[]{:S(2)}) async-start(bf16[4,2,64,256]{3,2,1,0:T(8,128)(2,1)} %bitcast.1), calls=%async_computation | async-start | bytes 524288 | tf_op jit(solution)/shard_map/all_to_all | solution.py:69
  19.7 0.6 copy-done.12
  20.3 0.1 iota_compare_fusion.1
  20.4 4.9 %collective-permute-done.1 = bf16[2,256,256]{2,1,0:T(8,128)(2,1)S(1)} collective-permute-done((bf16[2,256,256]{2,1,0:T(8,128)(2,1)}, bf16[2,256,256]{2,1,0:T(8,128)(2,1)S(1)}, u32[]{:S(2)}, u32[]{:S(2)}) %collective-permute-start.1) | collective-permute-done | bytes 262176 | tf_op jit(solution)/shard_map/ppermute | solution.py:17
  25.3 0.1 pad_maximum_fusion
  25.4 0.6 gather_fusion.1
  26.0 0.4 copy-done.2
  26.4 0.3 convolution_bitcast_fusion.4
  26.7 0.2 copy.67
  26.9 0.1 select_reduce_fusion.3
  27.1 0.2 copy.68
  27.3 2.8 %all-to-all-done = bf16[4,2,64,256]{3,2,1,0:T(8,128)(2,1)S(1)} async-done(((bf16[4,2,64,256]{3,2,1,0:T(8,128)(2,1)}), bf16[4,2,64,256]{3,2,1,0:T(8,128)(2,1)S(1)}, u32[]{:S(2)}, u32[]{:S(2)}) %all-to-all-start) | async-done | bytes 262176 | tf_op jit(solution)/shard_map/all_to_all | solution.py:69
  30.0 1.1 fusion.9
  31.2 0.1 copy.65
  31.3 32.5 %all-reduce.3.cloned.1.call-done = f32[2,256,256]{1,2,0:T(8,128)} async-done(((f32[2,256,256]{1,2,0:T(8,128)}), f32[2,256,256]{1,2,0:T(8,128)}) %all-reduce.3.cloned.1.call-update) | async-done | bytes 524304 | tf_op jit(solution)/shard_map/psum | solution.py:86
  63.8 1.1 add_convert_fusion.1
  64.9 1.5 collective-permute-start.2
  66.4 2.3 %collective-permute-start.3 = (bf16[2,256,256]{1,2,0:T(8,128)(2,1)S(1)}, bf16[2,256,256]{1,2,0:T(8,128)(2,1)S(1)}, u32[]{:S(2)}, u32[]{:S(2)}) collective-permute-start(bf16[2,256,256]{1,2,0:T(8,128)(2,1)S(1)} %add_convert_fusion.1), channel_id=1, source_target_pairs={{4,0},{8,4},{12,8},{0,12},{5,1},{9,5},{13,9},{1,13},{6,2},{10,6},{... | collective-permute-start | bytes 786440 | tf_op jit(solution)/shard_map/ppermute | solution.py:17
  68.7 0.6 gather_fusion.2
  69.4 1.2 fusion.11
  70.6 3.4 %all-to-all-start.1 = ((bf16[4,2,64,256]{3,2,1,0:T(8,128)(2,1)}), bf16[4,2,64,256]{3,2,1,0:T(8,128)(2,1)S(1)}, u32[]{:S(2)}, u32[]{:S(2)}) async-start(bf16[4,2,64,256]{3,2,1,0:T(8,128)(2,1)} %bitcast.7), calls=%async_computation.1 | async-start | bytes 524288 | tf_op jit(solution)/shard_map/all_to_all | solution.py:69
  74.0 0.0 all-reduce.5.cloned.1.call-start
  74.0 1.9 %collective-permute-done.2 = bf16[2,256,256]{1,2,0:T(8,128)(2,1)S(1)} collective-permute-done((bf16[2,256,256]{1,2,0:T(8,128)(2,1)S(1)}, bf16[2,256,256]{1,2,0:T(8,128)(2,1)S(1)}, u32[]{:S(2)}, u32[]{:S(2)}) %collective-permute-start.2) | collective-permute-done | bytes 262176 | tf_op jit(solution)/shard_map/ppermute | solution.py:14
  76.0 4.2 %collective-permute-done.3 = bf16[2,256,256]{1,2,0:T(8,128)(2,1)S(1)} collective-permute-done((bf16[2,256,256]{1,2,0:T(8,128)(2,1)S(1)}, bf16[2,256,256]{1,2,0:T(8,128)(2,1)S(1)}, u32[]{:S(2)}, u32[]{:S(2)}) %collective-permute-start.3) | collective-permute-done | bytes 262176 | tf_op jit(solution)/shard_map/ppermute | solution.py:17
  80.2 0.1 pad_maximum_fusion.1
  80.3 0.6 gather_fusion.3
  80.8 0.3 convolution_bitcast_fusion.2
  81.1 0.2 copy.70
  81.3 0.1 select_reduce_fusion.2
  81.4 0.2 copy.71
  81.7 3.2 %all-to-all-done.1 = bf16[4,2,64,256]{3,2,1,0:T(8,128)(2,1)S(1)} async-done(((bf16[4,2,64,256]{3,2,1,0:T(8,128)(2,1)}), bf16[4,2,64,256]{3,2,1,0:T(8,128)(2,1)S(1)}, u32[]{:S(2)}, u32[]{:S(2)}) %all-to-all-start.1) | async-done | bytes 262176 | tf_op jit(solution)/shard_map/all_to_all | solution.py:69
  84.9 1.1 fusion.10
  86.0 0.7 copy-done.6
  86.7 0.3 copy-done.3
  87.0 0.3 copy.72
  87.3 0.3 reshape.95
  87.7 0.3 copy-done.4
  88.0 0.1 copy.75
  88.1 0.5 copy-done.5
  88.7 29.0 %all-reduce.5.cloned.1.call-done = f32[2,256,256]{1,2,0:T(8,128)} async-done(((f32[2,256,256]{1,2,0:T(8,128)}), f32[2,256,256]{1,2,0:T(8,128)}) %all-reduce.5.cloned.1.call-update) | async-done | bytes 524304 | tf_op jit(solution)/shard_map/psum | solution.py:86
  117.7 1.1 add_convert_fusion
  118.8 0.3 convolution_bitcast_fusion.1
  119.1 1.2 convolution_bitcast_fusion
  120.3 0.8 copy.77
  121.1 0.3 copy.73
  121.4 0.3 reshape.96
  121.7 1.4 copy.74
  123.1 0.3 reshape.97
  123.5 2.9 %multiply_reduce_fusion.1 = (f32[256,256]{1,0:T(8,128)S(1)}, f32[256,3,256]{2,1,0:T(4,128)S(1)}) fusion(f32[256,3,256]{2,1,0:T(4,128)S(1)} %reshape.97, pred[256]{0:T(512)(128)(4,1)S(1)} %get-tuple-element.31, f32[256,3,256]{2,1,0:T(4,128)S(1)} %reshape.96, pred[256]{0:T(512)(128)(4,1)S(1)} %get-tuple-element.30), kind=kLoop, calls=%fused_computation.26 | loop fusion | flops 917504 | bytes 2621952 | tf_op jit(solution)/shard_map/reduce_sum | solution.py:42
  126.5 0.7 copy-done.8
  127.1 1.9 %select_reduce_fusion.1 = (f32[3,256]{1,0:T(4,128)S(1)}, f32[3,256]{1,0:T(4,128)S(1)}, f32[256,3,256]{2,1,0:T(4,128)S(1)}) fusion(pred[256]{0:T(512)(128)(4,1)S(1)} %get-tuple-element.30, pred[256]{0:T(512)(128)(4,1)S(1)} %get-tuple-element.31, f32[256]{0:T(256)S(1)} %copy-done.8, f32[256,3]{1,0:T(8,128)S(1)} %copy.75, ...), kind=kOutput, calls=%fused_computation.25 | output fusion | flops 1833474 | bytes 1845760 | tf_op jit(solution)/shard_map/mul | solution.py:43
  129.1 0.5 fusion.36
  129.6 0.2 fusion.25
  129.8 31.3 %psum.31 = f32[3,256]{1,0:T(4,128)S(1)} all-reduce(f32[3,256]{1,0:T(4,128)S(1)} %pad_maximum_fusion.3), channel_id=1, replica_groups=mesh['design'=2,'cluster'=4,'blk'=2,'sub'=2] {'cluster','blk','sub'}, use_global_device_ids=true, to_apply=%region_12.15 | all-reduce | flops 768 | bytes 6144 | tf_op jit(solution)/shard_map/psum | solution.py:116
  161.2 0.6 broadcast_multiply_fusion.1
  161.8 5.8 %psum.30 = f32[2,3,256]{2,1,0:T(4,128)S(1)} all-reduce(f32[2,3,256]{2,1,0:T(4,128)S(1)} %pad_maximum_fusion.2), channel_id=1, replica_groups=mesh['design'=2,'cluster'=4,'blk'=2,'sub'=2] {'blk','sub'}, use_global_device_ids=true, to_apply=%region_8.11 | all-reduce | flops 1536 | bytes 12288 | tf_op jit(solution)/shard_map/psum | solution.py:115
  167.6 0.6 copy.78
  (33 shorter events, 0.2 us)
Async XLA Ops:
  7.2 22.9 %copy-start = (bf16[8,64,256]{2,1,0:T(8,128)(2,1)S(1)}, bf16[8,64,256]{2,1,0:T(8,128)(2,1)}, u32[]{:S(2)}) copy-start(bf16[8,64,256]{2,1,0:T(8,128)(2,1)} %param.21) | copy-start | bytes 786436
  7.2 5.8 %copy-start.9 = (s32[8]{0:T(128)S(1)}, s32[8]{0:T(128)}, u32[]{:S(2)}) copy-start(s32[8]{0:T(128)} %param.18) | copy-start | bytes 100
  7.2 13.2 %collective-permute-start = (bf16[2,256,256]{2,1,0:T(8,128)(2,1)}, bf16[2,256,256]{2,1,0:T(8,128)(2,1)S(1)}, u32[]{:S(2)}, u32[]{:S(2)}) collective-permute-start(bf16[2,256,256]{2,1,0:T(8,128)(2,1)} %param.17), channel_id=1, source_target_pairs={{0,4},{4,8},{8,12},{12,0},{1,5},{5,9},{9,13},{13,1},{2,6},{6,10},{... | collective-permute-start | bytes 786440 | tf_op jit(solution)/shard_map/ppermute | solution.py:14
  10.3 15.1 %collective-permute-start.1 = (bf16[2,256,256]{2,1,0:T(8,128)(2,1)}, bf16[2,256,256]{2,1,0:T(8,128)(2,1)S(1)}, u32[]{:S(2)}, u32[]{:S(2)}) collective-permute-start(bf16[2,256,256]{2,1,0:T(8,128)(2,1)} %param.17), channel_id=1, source_target_pairs={{4,0},{8,4},{12,8},{0,12},{5,1},{9,5},{13,9},{1,13},{6,2},{10,6},{... | collective-permute-start | bytes 786440 | tf_op jit(solution)/shard_map/ppermute | solution.py:17
  13.0 1.6 copy-start.10
  13.1 1.8 %copy-start.7 = (bf16[8,64,256]{2,1,0:T(8,128)(2,1)S(1)}, bf16[8,64,256]{2,1,0:T(8,128)(2,1)}, u32[]{:S(2)}) copy-start(bf16[8,64,256]{2,1,0:T(8,128)(2,1)} %param.20) | copy-start | bytes 786436
  16.0 3.6 %copy-start.11 = (s32[2]{0:T(128)S(1)}, s32[2]{0:T(128)}, u32[]{:S(2)}) copy-start(s32[2]{0:T(128)} %param.23) | copy-start | bytes 28
  16.0 9.3 %copy-start.1 = (bf16[2,256,256]{2,1,0:T(8,128)(2,1)S(1)}, bf16[2,256,256]{2,1,0:T(8,128)(2,1)}, u32[]{:S(2)}) copy-start(bf16[2,256,256]{2,1,0:T(8,128)(2,1)} %param.17) | copy-start | bytes 786436
  16.0 14.0 %all-to-all-start = ((bf16[4,2,64,256]{3,2,1,0:T(8,128)(2,1)}), bf16[4,2,64,256]{3,2,1,0:T(8,128)(2,1)S(1)}, u32[]{:S(2)}, u32[]{:S(2)}) async-start(bf16[4,2,64,256]{3,2,1,0:T(8,128)(2,1)} %bitcast.1), calls=%async_computation | async-start | bytes 524288 | tf_op jit(solution)/shard_map/all_to_all | solution.py:69
  19.6 44.2 %all-reduce.3.cloned.1.call-start = ((), (), s32[]{:S(2)}) async-start(), calls=%async_computation.2 | async-start | bytes 1048576 | tf_op jit(solution)/shard_map/psum | solution.py:86
  19.7 0.7 copy-start.12
  25.4 1.0 copy-start.2
  64.9 11.1 %collective-permute-start.2 = (bf16[2,256,256]{1,2,0:T(8,128)(2,1)S(1)}, bf16[2,256,256]{1,2,0:T(8,128)(2,1)S(1)}, u32[]{:S(2)}, u32[]{:S(2)}) collective-permute-start(bf16[2,256,256]{1,2,0:T(8,128)(2,1)S(1)} %add_convert_fusion.1), channel_id=1, source_target_pairs={{0,4},{4,8},{8,12},{12,0},{1,5},{5,9},{9,13},{13,1},{2,6},{6,10},{... | collective-permute-start | bytes 786440 | tf_op jit(solution)/shard_map/ppermute | solution.py:14
  66.4 13.8 %collective-permute-start.3 = (bf16[2,256,256]{1,2,0:T(8,128)(2,1)S(1)}, bf16[2,256,256]{1,2,0:T(8,128)(2,1)S(1)}, u32[]{:S(2)}, u32[]{:S(2)}) collective-permute-start(bf16[2,256,256]{1,2,0:T(8,128)(2,1)S(1)} %add_convert_fusion.1), channel_id=1, source_target_pairs={{4,0},{8,4},{12,8},{0,12},{5,1},{9,5},{13,9},{1,13},{6,2},{10,6},{... | collective-permute-start | bytes 786440 | tf_op jit(solution)/shard_map/ppermute | solution.py:17
  70.6 14.3 %all-to-all-start.1 = ((bf16[4,2,64,256]{3,2,1,0:T(8,128)(2,1)}), bf16[4,2,64,256]{3,2,1,0:T(8,128)(2,1)S(1)}, u32[]{:S(2)}, u32[]{:S(2)}) async-start(bf16[4,2,64,256]{3,2,1,0:T(8,128)(2,1)} %bitcast.7), calls=%async_computation.1 | async-start | bytes 524288 | tf_op jit(solution)/shard_map/all_to_all | solution.py:69
  74.0 43.7 %all-reduce.5.cloned.1.call-start = ((), (), s32[]{:S(2)}) async-start(), calls=%async_computation.3 | async-start | bytes 1048576 | tf_op jit(solution)/shard_map/psum | solution.py:86
  86.0 1.0 copy-start.3
  86.0 0.7 copy-start.6
  87.3 0.7 copy-start.4
  88.0 0.7 copy-start.5
  126.4 0.7 copy-start.8
Sparse Core Ops, SparseCore 0:
  31.3 32.4 all-reduce.2
  86.1 31.5 all-reduce.4
where the time goes:
time: 176 us; the launch traced here: 175 us
  waiting for transfers between devices  78.5 us (45%)
  blocking collectives  37.2 us (21%)
  starting transfers between devices  16.1 us (9%)
  between operations  14.4 us (8%)
  local copies, waits for them, and re-layouts  13 us (7%)
  other arithmetic  9.29 us (5%)
  matrix products  6.61 us (4%)
    psum x2, waiting for transfers between devices, apply_operator(): summed = lax.psum(partial_sum, ('blk', 'sub'))  61.5 us
    psum x1, blocking collectives, per_device(): torque = lax.psum(torque_part, ('cluster', 'blk', 'sub'))  31.3 us
    ppermute x2, waiting for transfers between devices, padded(): lax.ppermute(lax.slice_in_dim(block, 0, width, axis=dim), axis, backward)  9.12 us
    all_to_all x2, starting transfers between devices, far_field(): lax.all_to_all(coeffs, 'cluster', split_axis=0, concat_axis=0, tiled=True)  6.95 us
    all_to_all x2, waiting for transfers between devices, far_field(): lax.all_to_all(coeffs, 'cluster', split_axis=0, concat_axis=0, tiled=True)  5.97 us
    psum x1, blocking collectives, per_device(): sector_force = lax.psum(sector_part, ('blk', 'sub'))  5.84 us
    unnamed x30, local copies, waits for them, and re-layouts  5.5 us
    ppermute x2, starting transfers between devices, padded(): lax.ppermute(lax.slice_in_dim(block, block.shape[dim] - width, None, axis...  4.62 us
  transfers between devices with their start and end apart: 8, of which 7 were waited for; matrix products, arithmetic and copies ran while one was open for 5% of the time, Pallas kernels for 0%

commit v1 on v0

--- a/solution.py
+++ b/solution.py
@@ -83,7 +83,7 @@
     partial_sum = far_field(field, far_cols, far_bucket, far_v, far_u) + near_field(
         field, near_rows, near_cols, near_tiles
     )
-    summed = lax.psum(partial_sum, ("blk", "sub"))
+    summed = lax.psum(lax.psum(partial_sum, "sub"), "blk")
     return (0.5 * field.astype(jnp.float32) + summed).astype(jnp.bfloat16)
 
 

time: 176 us -> 213 us (1.21)
  waiting for transfers between devices: 78.5 us -> 116 us
    psum x2 -> x4, waiting for transfers between devices: 61.5 us -> 97.4 us  [apply_operator(): summed = lax.psum(lax.psum(partial_sum, 'sub'), 'blk')]
  transfers between devices with their start and end apart: 8 -> 10, of which waited for: 7 -> 9; matrix products, arithmetic and copies ran while one was open for 5% -> 4% of each run, Pallas kernels for 0% -> 0%
where the time goes in v1:
time: 213 us; the launch traced here: 212 us
  waiting for transfers between devices  116 us (54%)
  blocking collectives  38.1 us (18%)
  starting transfers between devices  16.2 us (8%)
  between operations  14.1 us (7%)
  local copies, waits for them, and re-layouts  12 us (6%)
  other arithmetic  9.29 us (4%)
  matrix products  6.61 us (3%)
    psum x4, waiting for transfers between devices, apply_operator(): summed = lax.psum(lax.psum(partial_sum, 'sub'), 'blk')  97.4 us
    psum x1, blocking collectives, per_device(): torque = lax.psum(torque_part, ('cluster', 'blk', 'sub'))  32.2 us
    ppermute x2, waiting for transfers between devices, padded(): lax.ppermute(lax.slice_in_dim(block, 0, width, axis=dim), axis, backward)  10.2 us
    all_to_all x2, starting transfers between devices, far_field(): lax.all_to_all(coeffs, 'cluster', split_axis=0, concat_axis=0, tiled=True)  6.95 us
    all_to_all x2, waiting for transfers between devices, far_field(): lax.all_to_all(coeffs, 'cluster', split_axis=0, concat_axis=0, tiled=True)  6.07 us
    psum x1, blocking collectives, per_device(): sector_force = lax.psum(sector_part, ('blk', 'sub'))  5.84 us
    ppermute x2, starting transfers between devices, padded(): lax.ppermute(lax.slice_in_dim(block, block.shape[dim] - width, None, axis...  4.61 us
    unnamed x30, local copies, waits for them, and re-layouts  4.51 us
  transfers between devices with their start and end apart: 10, of which 9 were waited for; matrix products, arithmetic and copies ran while one was open for 4% of the time, Pallas kernels for 0%

profile of v1, /device:TPU:0, one launch (start us, length us, event | category | flops | bytes accessed | tf_op | source)
XLA Modules:
  0.0 212.0 jit_solution(5001747654381461495)
XLA Ops:
  7.2 3.1 %collective-permute-start = (bf16[2,256,256]{2,1,0:T(8,128)(2,1)}, bf16[2,256,256]{2,1,0:T(8,128)(2,1)S(1)}, u32[]{:S(2)}, u32[]{:S(2)}) collective-permute-start(bf16[2,256,256]{2,1,0:T(8,128)(2,1)} %param.17), channel_id=1, source_target_pairs={{0,4},{4,8},{8,12},{12,0},{1,5},{5,9},{9,13},{13,1},{2,6},{6,10},{... | collective-permute-start | bytes 786440 | tf_op jit(solution)/shard_map/ppermute | solution.py:14
  10.3 2.1 collective-permute-start.1
  12.4 0.7 compare_select_fusion.1
  13.1 1.6 gather_fusion
  14.7 0.1 compare_select_fusion.2
  14.8 0.1 iota_compare_fusion
  14.9 1.1 fusion.12
  16.0 3.5 %all-to-all-start = ((bf16[4,2,64,256]{3,2,1,0:T(8,128)(2,1)}), bf16[4,2,64,256]{3,2,1,0:T(8,128)(2,1)S(1)}, u32[]{:S(2)}, u32[]{:S(2)}) async-start(bf16[4,2,64,256]{3,2,1,0:T(8,128)(2,1)} %bitcast.1), calls=%async_computation | async-start | bytes 524288 | tf_op jit(solution)/shard_map/all_to_all | solution.py:69
  19.7 0.6 copy-done.12
  20.3 0.1 iota_compare_fusion.1
  20.4 4.9 %collective-permute-done.1 = bf16[2,256,256]{2,1,0:T(8,128)(2,1)S(1)} collective-permute-done((bf16[2,256,256]{2,1,0:T(8,128)(2,1)}, bf16[2,256,256]{2,1,0:T(8,128)(2,1)S(1)}, u32[]{:S(2)}, u32[]{:S(2)}) %collective-permute-start.1) | collective-permute-done | bytes 262176 | tf_op jit(solution)/shard_map/ppermute | solution.py:17
  25.3 0.1 pad_maximum_fusion
  25.4 0.6 gather_fusion.1
  26.0 0.4 copy-done.2
  26.4 0.3 convolution_bitcast_fusion.4
  26.7 0.2 copy.67
  26.9 0.1 select_reduce_fusion.3
  27.1 0.2 copy.68
  27.3 2.8 %all-to-all-done = bf16[4,2,64,256]{3,2,1,0:T(8,128)(2,1)S(1)} async-done(((bf16[4,2,64,256]{3,2,1,0:T(8,128)(2,1)}), bf16[4,2,64,256]{3,2,1,0:T(8,128)(2,1)S(1)}, u32[]{:S(2)}, u32[]{:S(2)}) %all-to-all-start) | async-done | bytes 262176 | tf_op jit(solution)/shard_map/all_to_all | solution.py:69
  30.0 1.1 fusion.9
  31.2 0.0 all-reduce.7.cloned.1.call-start
  31.2 18.1 %all-reduce.5.cloned.1.call-done = f32[2,256,256]{1,2,0:T(8,128)} async-done(((f32[2,256,256]{1,2,0:T(8,128)}), f32[2,256,256]{1,2,0:T(8,128)}) %all-reduce.5.cloned.1.call-update) | async-done | bytes 524304 | tf_op jit(solution)/shard_map/psum | solution.py:86
  49.3 0.1 copy.65
  49.5 32.0 %all-reduce.7.cloned.1.call-done = f32[2,256,256]{1,2,0:T(8,128)} async-done(((f32[2,256,256]{1,2,0:T(8,128)}), f32[2,256,256]{1,2,0:T(8,128)}) %all-reduce.7.cloned.1.call-update) | async-done | bytes 524304 | tf_op jit(solution)/shard_map/psum | solution.py:86
  81.5 1.1 add_convert_fusion.1
  82.6 1.5 collective-permute-start.2
  84.2 2.3 %collective-permute-start.3 = (bf16[2,256,256]{1,2,0:T(8,128)(2,1)S(1)}, bf16[2,256,256]{1,2,0:T(8,128)(2,1)S(1)}, u32[]{:S(2)}, u32[]{:S(2)}) collective-permute-start(bf16[2,256,256]{1,2,0:T(8,128)(2,1)S(1)} %add_convert_fusion.1), channel_id=1, source_target_pairs={{4,0},{8,4},{12,8},{0,12},{5,1},{9,5},{13,9},{1,13},{6,2},{10,6},{... | collective-permute-start | bytes 786440 | tf_op jit(solution)/shard_map/ppermute | solution.py:17
  86.5 0.6 gather_fusion.2
  87.1 1.2 fusion.11
  88.3 3.4 %all-to-all-start.1 = ((bf16[4,2,64,256]{3,2,1,0:T(8,128)(2,1)}), bf16[4,2,64,256]{3,2,1,0:T(8,128)(2,1)S(1)}, u32[]{:S(2)}, u32[]{:S(2)}) async-start(bf16[4,2,64,256]{3,2,1,0:T(8,128)(2,1)} %bitcast.7), calls=%async_computation.1 | async-start | bytes 524288 | tf_op jit(solution)/shard_map/all_to_all | solution.py:69
  91.8 1.9 collective-permute-done.2
  93.7 5.2 %collective-permute-done.3 = bf16[2,256,256]{1,2,0:T(8,128)(2,1)S(1)} collective-permute-done((bf16[2,256,256]{1,2,0:T(8,128)(2,1)S(1)}, bf16[2,256,256]{1,2,0:T(8,128)(2,1)S(1)}, u32[]{:S(2)}, u32[]{:S(2)}) %collective-permute-start.3) | collective-permute-done | bytes 262176 | tf_op jit(solution)/shard_map/ppermute | solution.py:17
  98.9 0.1 pad_maximum_fusion.1
  99.0 0.6 gather_fusion.3
  99.6 0.3 convolution_bitcast_fusion.2
  99.9 0.2 copy.70
  100.1 0.1 select_reduce_fusion.2
  100.2 0.2 copy.71
  100.4 3.3 %all-to-all-done.1 = bf16[4,2,64,256]{3,2,1,0:T(8,128)(2,1)S(1)} async-done(((bf16[4,2,64,256]{3,2,1,0:T(8,128)(2,1)}), bf16[4,2,64,256]{3,2,1,0:T(8,128)(2,1)S(1)}, u32[]{:S(2)}, u32[]{:S(2)}) %all-to-all-start.1) | async-done | bytes 262176 | tf_op jit(solution)/shard_map/all_to_all | solution.py:69
  103.8 1.1 fusion.10
  104.9 17.0 %all-reduce.9.cloned.1.call-done = f32[2,256,256]{1,2,0:T(8,128)} async-done(((f32[2,256,256]{1,2,0:T(8,128)}), f32[2,256,256]{1,2,0:T(8,128)}) %all-reduce.9.cloned.1.call-update) | async-done | bytes 524304 | tf_op jit(solution)/shard_map/psum | solution.py:86
  122.0 0.3 copy.72
  122.4 0.3 reshape.95
  122.7 0.3 copy-done.4
  123.0 0.1 copy.75
  123.2 0.5 copy-done.6
  123.7 30.3 %all-reduce.11.cloned.1.call-done = f32[2,256,256]{1,2,0:T(8,128)} async-done(((f32[2,256,256]{1,2,0:T(8,128)}), f32[2,256,256]{1,2,0:T(8,128)}) %all-reduce.11.cloned.1.call-update) | async-done | bytes 524304 | tf_op jit(solution)/shard_map/psum | solution.py:86
  154.0 1.1 add_convert_fusion
  155.1 0.3 convolution_bitcast_fusion.1
  155.4 1.2 convolution_bitcast_fusion
  156.6 0.8 copy.77
  157.4 0.3 copy.73
  157.7 0.3 reshape.96
  158.0 1.4 copy.74
  159.5 0.3 reshape.97
  159.8 2.9 %multiply_reduce_fusion.1 = (f32[256,256]{1,0:T(8,128)S(1)}, f32[256,3,256]{2,1,0:T(4,128)S(1)}) fusion(f32[256,3,256]{2,1,0:T(4,128)S(1)} %reshape.97, pred[256]{0:T(512)(128)(4,1)S(1)} %get-tuple-element.31, f32[256,3,256]{2,1,0:T(4,128)S(1)} %reshape.96, pred[256]{0:T(512)(128)(4,1)S(1)} %get-tuple-element.30), kind=kLoop, calls=%fused_computation.26 | loop fusion | flops 917504 | bytes 2621952 | tf_op jit(solution)/shard_map/reduce_sum | solution.py:42
  162.8 0.7 copy-done.8
  163.4 1.9 select_reduce_fusion.1
  165.4 0.5 fusion.36
  165.9 0.2 fusion.25
  166.1 32.2 %psum.47 = f32[3,256]{1,0:T(4,128)S(1)} all-reduce(f32[3,256]{1,0:T(4,128)S(1)} %pad_maximum_fusion.3), channel_id=1, replica_groups=mesh['design'=2,'cluster'=4,'blk'=2,'sub'=2] {'cluster','blk','sub'}, use_global_device_ids=true, to_apply=%region_14.17 | all-reduce | flops 768 | bytes 6144 | tf_op jit(solution)/shard_map/psum | solution.py:116
  198.4 0.6 broadcast_multiply_fusion.1
  199.0 5.8 %psum.46 = f32[2,3,256]{2,1,0:T(4,128)S(1)} all-reduce(f32[2,3,256]{2,1,0:T(4,128)S(1)} %pad_maximum_fusion.2), channel_id=1, replica_groups=mesh['design'=2,'cluster'=4,'blk'=2,'sub'=2] {'blk','sub'}, use_global_device_ids=true, to_apply=%region_10.13 | all-reduce | flops 1536 | bytes 12288 | tf_op jit(solution)/shard_map/psum | solution.py:115
  204.8 0.6 copy.78
  (39 shorter events, 0.3 us)
Async XLA Ops:
  7.2 22.9 %copy-start = (bf16[8,64,256]{2,1,0:T(8,128)(2,1)S(1)}, bf16[8,64,256]{2,1,0:T(8,128)(2,1)}, u32[]{:S(2)}) copy-start(bf16[8,64,256]{2,1,0:T(8,128)(2,1)} %param.21) | copy-start | bytes 786436
  7.2 5.8 %copy-start.9 = (s32[8]{0:T(128)S(1)}, s32[8]{0:T(128)}, u32[]{:S(2)}) copy-start(s32[8]{0:T(128)} %param.18) | copy-start | bytes 100
  7.2 13.2 %collective-permute-start = (bf16[2,256,256]{2,1,0:T(8,128)(2,1)}, bf16[2,256,256]{2,1,0:T(8,128)(2,1)S(1)}, u32[]{:S(2)}, u32[]{:S(2)}) collective-permute-start(bf16[2,256,256]{2,1,0:T(8,128)(2,1)} %param.17), channel_id=1, source_target_pairs={{0,4},{4,8},{8,12},{12,0},{1,5},{5,9},{9,13},{13,1},{2,6},{6,10},{... | collective-permute-start | bytes 786440 | tf_op jit(solution)/shard_map/ppermute | solution.py:14
  10.3 15.1 %collective-permute-start.1 = (bf16[2,256,256]{2,1,0:T(8,128)(2,1)}, bf16[2,256,256]{2,1,0:T(8,128)(2,1)S(1)}, u32[]{:S(2)}, u32[]{:S(2)}) collective-permute-start(bf16[2,256,256]{2,1,0:T(8,128)(2,1)} %param.17), channel_id=1, source_target_pairs={{4,0},{8,4},{12,8},{0,12},{5,1},{9,5},{13,9},{1,13},{6,2},{10,6},{... | collective-permute-start | bytes 786440 | tf_op jit(solution)/shard_map/ppermute | solution.py:17
  13.0 1.6 copy-start.10
  13.1 1.8 copy-start.7
  16.0 3.6 %copy-start.11 = (s32[2]{0:T(128)S(1)}, s32[2]{0:T(128)}, u32[]{:S(2)}) copy-start(s32[2]{0:T(128)} %param.23) | copy-start | bytes 28
  16.0 9.3 %copy-start.1 = (bf16[2,256,256]{2,1,0:T(8,128)(2,1)S(1)}, bf16[2,256,256]{2,1,0:T(8,128)(2,1)}, u32[]{:S(2)}) copy-start(bf16[2,256,256]{2,1,0:T(8,128)(2,1)} %param.17) | copy-start | bytes 786436
  16.0 14.0 %all-to-all-start = ((bf16[4,2,64,256]{3,2,1,0:T(8,128)(2,1)}), bf16[4,2,64,256]{3,2,1,0:T(8,128)(2,1)S(1)}, u32[]{:S(2)}, u32[]{:S(2)}) async-start(bf16[4,2,64,256]{3,2,1,0:T(8,128)(2,1)} %bitcast.1), calls=%async_computation | async-start | bytes 524288 | tf_op jit(solution)/shard_map/all_to_all | solution.py:69
  19.6 29.7 %all-reduce.5.cloned.1.call-start = ((), (), s32[]{:S(2)}) async-start(), calls=%async_computation.2 | async-start | bytes 1048576 | tf_op jit(solution)/shard_map/psum | solution.py:86
  19.7 0.7 copy-start.12
  25.4 1.0 copy-start.2
  31.2 50.3 %all-reduce.7.cloned.1.call-start = ((), (), s32[]{:S(2)}) async-start(), calls=%async_computation.3 | async-start | bytes 1048576 | tf_op jit(solution)/shard_map/psum | solution.py:86
  82.6 11.1 %collective-permute-start.2 = (bf16[2,256,256]{1,2,0:T(8,128)(2,1)S(1)}, bf16[2,256,256]{1,2,0:T(8,128)(2,1)S(1)}, u32[]{:S(2)}, u32[]{:S(2)}) collective-permute-start(bf16[2,256,256]{1,2,0:T(8,128)(2,1)S(1)} %add_convert_fusion.1), channel_id=1, source_target_pairs={{0,4},{4,8},{8,12},{12,0},{1,5},{5,9},{9,13},{13,1},{2,6},{6,10},{... | collective-permute-start | bytes 786440 | tf_op jit(solution)/shard_map/ppermute | solution.py:14
  84.2 14.8 %collective-permute-start.3 = (bf16[2,256,256]{1,2,0:T(8,128)(2,1)S(1)}, bf16[2,256,256]{1,2,0:T(8,128)(2,1)S(1)}, u32[]{:S(2)}, u32[]{:S(2)}) collective-permute-start(bf16[2,256,256]{1,2,0:T(8,128)(2,1)S(1)} %add_convert_fusion.1), channel_id=1, source_target_pairs={{4,0},{8,4},{12,8},{0,12},{5,1},{9,5},{13,9},{1,13},{6,2},{10,6},{... | collective-permute-start | bytes 786440 | tf_op jit(solution)/shard_map/ppermute | solution.py:17
  88.3 15.4 %all-to-all-start.1 = ((bf16[4,2,64,256]{3,2,1,0:T(8,128)(2,1)}), bf16[4,2,64,256]{3,2,1,0:T(8,128)(2,1)S(1)}, u32[]{:S(2)}, u32[]{:S(2)}) async-start(bf16[4,2,64,256]{3,2,1,0:T(8,128)(2,1)} %bitcast.7), calls=%async_computation.1 | async-start | bytes 524288 | tf_op jit(solution)/shard_map/all_to_all | solution.py:69
  91.7 30.2 %all-reduce.9.cloned.1.call-start = ((), (), s32[]{:S(2)}) async-start(), calls=%async_computation.4 | async-start | bytes 1048576 | tf_op jit(solution)/shard_map/psum | solution.py:86
  104.9 17.1 %copy-start.3 = (bf16[256,3,256]{2,0,1:T(8,128)(2,1)S(1)}, bf16[256,3,256]{2,0,1:T(8,128)(2,1)}, u32[]{:S(2)}) copy-start(bf16[256,3,256]{2,0,1:T(8,128)(2,1)} %param.26) | copy-start | bytes 1179652
  104.9 49.1 %all-reduce.11.cloned.1.call-start = ((), (), s32[]{:S(2)}) async-start(), calls=%async_computation.5 | async-start | bytes 1048576 | tf_op jit(solution)/shard_map/psum | solution.py:86
  122.3 0.7 copy-start.4
  122.3 1.4 copy-start.5
  123.0 0.7 copy-start.6
  162.7 0.7 copy-start.8
Sparse Core Ops, SparseCore 0:
  31.3 17.9 all-reduce.4
  51.7 29.7 all-reduce.6
  105.0 16.9 all-reduce.8
  124.2 29.7 all-reduce.10
